TPU v7x, 32 devices: a whole 2x2x4 slice. The times are simulated.
32 devices in a mesh: wide: 16 (over z, y, core), rep: 2 (over x).
Axes of the slice: x: 2, y: 2, z: 4, core: 2. Of those that a mesh axis runs over, the one named last changes fastest.
Arguments:
- features: bfloat16 [4096, 512], P(('wide', 'rep')), may hold values from -6 to 6
- w_query: bfloat16 [512, 512], replicated, may hold values from -0.25 to 0.25
- w_key: bfloat16 [512, 512], replicated, may hold values from -0.25 to 0.25
- w_out: bfloat16 [512, 512], replicated, may hold values from -0.25 to 0.25
- edge_weight: bfloat16 [16, 2, 6, 128, 128], P('wide', 'rep'), may hold values from -0.23925781 to 0.23925781
- tile_slot: int32 [16, 2, 6], P('wide', 'rep'), may hold values from 0 to 31, as said below
- tile_count: int32 [16, 2], P('wide', 'rep'), may hold values from 1 to 6, as said below
Outputs:
- updated: bfloat16 [4096, 512], P(('wide', 'rep'))
Inputs may be any that keep to these rules, and one draw needn't show every extreme that they name: For each w and r the first tile_count[w, r] entries of tile_slot[w, r] are distinct and ascending; all 6 entries of a list are distinct. `tile_count`: some device has 6 live tiles.
All inputs are finite; a program needn't handle non-finite values.
Results may differ from a plain program's by a relative error of at most 0.014.
Values may be sent and summed in bfloat16 or wider, within the bound.
No kernel may reach another device: no remote copies, remote signals or barrier semaphores. Data moves between devices by JAX's collectives and lax.ppermute only.
A program may use at most 64 MiB of HBM per device.

v0:
```python
import jax
import jax.numpy as jnp
from jax import lax
from jax.sharding import PartitionSpec as P


def on_device(features, w_query, w_key, w_out, edge_weight, tile_slot, tile_count):
    tile_rows = features.shape[0]
    feat_width = features.shape[1]
    n_wide = lax.axis_size("wide")
    n_rep = lax.axis_size("rep")
    wide_pos = lax.axis_index("wide")
    query_rows = jnp.dot(features, w_query, preferred_element_type=jnp.float32).astype(jnp.bfloat16)
    key_rows = jnp.dot(features, w_key, preferred_element_type=jnp.float32).astype(jnp.bfloat16)
    receivers = lax.all_gather(query_rows, "rep", axis=0, tiled=True)
    tile_slots = tile_slot[0, 0]
    live_count = tile_count[0, 0]
    weights = edge_weight[0, 0]
    step_of = tile_slots // n_rep
    active = jnp.arange(tile_slots.shape[0], dtype=jnp.int32) < live_count
    below = step_of[None, :] < jnp.arange(n_wide + 1, dtype=jnp.int32)[:, None]
    bounds = jnp.sum((active[None, :] & below).astype(jnp.int32), axis=1)
    factor = 1.0 / float(feat_width) ** 0.5

    def one_tile(tile_num, sender, partial_value):
        block = tile_slots[tile_num] % n_rep
        targets = lax.dynamic_slice_in_dim(receivers, block * tile_rows, tile_rows, 0)
        scores = (
            lax.dot_general(
                targets, sender, (((1,), (1,)), ((), ())), preferred_element_type=jnp.float32
            )
            * factor
        )
        weighted = (jnp.tanh(scores) * weights[tile_num].astype(jnp.float32)).astype(jnp.bfloat16)
        contrib = jnp.dot(weighted, sender, preferred_element_type=jnp.float32)
        previous = lax.dynamic_slice_in_dim(partial_value, block * tile_rows, tile_rows, 0)
        return lax.dynamic_update_slice_in_dim(
            partial_value, previous + contrib, block * tile_rows, 0
        )

    def one_step(step_num, sender, partial_value):
        return lax.fori_loop(
            bounds[step_num],
            bounds[step_num + 1],
            lambda tile_num, acc: one_tile(tile_num, sender, acc),
            partial_value,
        )

    partial_value = jnp.zeros((n_rep * tile_rows, feat_width), jnp.float32)
    portion = lax.all_gather(key_rows, "wide", axis=0, tiled=True)

    def per_shard(index_in, inner):
        sender = lax.dynamic_slice_in_dim(portion, index_in * tile_rows, tile_rows, 0)
        return one_step((wide_pos - index_in) % n_wide, sender, inner)

    partial_value = lax.fori_loop(0, portion.shape[0] // tile_rows, per_shard, partial_value)
    summed = lax.psum_scatter(
        partial_value.astype(jnp.bfloat16), "rep", scatter_dimension=0, tiled=True
    )
    mixed = features.astype(jnp.float32) + jnp.dot(
        summed, w_out, preferred_element_type=jnp.float32
    )
    return mixed.astype(jnp.bfloat16)


def solution(mesh):
    in_specs = (
        P(("wide", "rep"), None),
        P(),
        P(),
        P(),
        P("wide", "rep", None, None, None),
        P("wide", "rep", None),
        P("wide", "rep"),
    )
    out_specs = P(("wide", "rep"), None)
    return jax.shard_map(
        on_device, mesh=mesh, in_specs=in_specs, out_specs=out_specs, check_vma=False
    )
```

profile of v0, /device:TPU:0, one launch (start us, length us, event | category | flops | bytes accessed | tf_op | source)
XLA Modules:
  0.0 158.1 jit_solution(510229438709745750)
XLA Ops:
  7.6 1.8 %convolution_convert_fusion.1 = bf16[128,512]{1,0:T(8,128)(2,1)} fusion(bf16[128,512]{1,0:T(8,128)(2,1)} %param.11, bf16[512,512]{1,0:T(8,128)(2,1)S(1)} %copy-done), kind=kOutput, calls=%fused_computation.17 | convolution fusion | flops 67174400 | bytes 786432 | tf_op jit(solution)/shard_map/dot_general | solution.py:14
  10.1 1.3 convolution_convert_fusion
  11.4 7.1 %all_gather.7 = bf16[256,512]{1,0:T(8,128)(2,1)S(1)} all-gather(bf16[128,512]{1,0:T(8,128)(2,1)S(1)} %convolution_convert_fusion), channel_id=1, replica_groups=mesh['wide'=16,'rep'=2] {'rep'}, dimensions={0}, use_global_device_ids=true | all-gather | bytes 393216 | tf_op jit(solution)/shard_map/all_gather | solution.py:15
  18.6 35.0 %all-gather.2.cloned.1.call-done = bf16[2048,512]{1,0:T(8,128)(2,1)} async-done(((bf16[128,512]{1,0:T(8,128)(2,1)}), bf16[2048,512]{1,0:T(8,128)(2,1)}) %all-gather.2.cloned.1.call-update) | async-done | bytes 2097168 | tf_op jit(solution)/shard_map/all_gather | solution.py:50
  53.8 53.0 %while.44 = (s32[]{:T(128)}, f32[256,512]{1,0:T(8,128)S(1)}, s32[]{:T(128)}, s32[17]{0:T(128)S(1)}, bf16[2048,512]{1,0:T(8,128)(2,1)}, /*index=5*/s32[6]{0:T(128...) while((s32[]{:T(128)}, f32[256,512]{1,0:T(8,128)S(1)}, ...), condition=%wide.region_4.5_spmd, body=%wide.region_1.4_spmd.sunk | while | flops 33685548 | bytes 1214878 | solution.py:56
  55.4 1.3 while.45
  58.3 7.6 %while.45 = (s32[]{:T(128)}, f32[256,512]{1,0:T(8,128)S(1)}, s32[]{:T(128)}, s32[6]{0:T(128)S(1)}, bf16[256,512]{1,0:T(8,128)(2,1)S(1)}, /*index=5*/bf16[128,512...) while((s32[]{:T(128)}, f32[256,512]{1,0:T(8,128)S(1)}, ...), condition=%wide.region_3.3_spmd, body=%wide.region_2.2_spmd.sunk | while | flops 33685524 | bytes 952142 | solution.py:42
  62.9 1.1 fusion.33
  67.5 1.3 while.45
  70.4 1.3 while.45
  73.3 1.3 while.45
  76.3 1.3 while.45
  79.2 1.3 while.45
  82.1 1.3 while.45
  85.0 1.3 while.45
  87.9 1.3 while.45
  90.8 1.3 while.45
  93.8 1.3 while.45
  96.7 1.3 while.45
  99.6 1.3 while.45
  102.5 1.3 while.45
  105.4 1.3 while.45
  107.5 42.0 %reduce-scatter.2.cloned.1.call-done = bf16[128,512]{1,0:T(8,128)(2,1)} async-done(((bf16[256,512]{1,0:T(8,128)(2,1)}), bf16[128,512]{1,0:T(8,128)(2,1)}) %reduce-scatter.2.cloned.1.call-update) | async-done | bytes 131088 | tf_op jit(solution)/shard_map/reduce_scatter | solution.py:57
  149.5 1.8 %fusion.13 = bf16[128,512]{1,0:T(8,128)(2,1)} fusion(bf16[128,512]{1,0:T(8,128)(2,1)} %reduce-scatter.2.cloned.1.call-done, bf16[512,512]{1,0:T(8,128)(2,1)S(1)} %copy-done.2, bf16[128,512]{1,0:T(8,128)(2,1)S(1)} %copy-done.1), kind=kOutput, calls=%fused_computation.15 | convolution fusion | flops 67305472 | bytes 917504 | tf_op jit(solution)/shard_map/dot_general | solution.py:60
  (50 shorter events, 27.8 us)
Async XLA Ops:
  6.5 1.0 copy-start
  6.5 12.0 %copy-start.3 = (s32[1,1,6]{2,1,0:T(1,128)S(1)}, s32[1,1,6]{2,1,0:T(1,128)}, u32[]{:S(2)}) copy-start(s32[1,1,6]{2,1,0:T(1,128)} %param.16) | copy-start | bytes 76
  6.5 47.1 %all-gather.2.cloned.1.call-start = ((), (), s32[]{:S(2)}) async-start(), calls=%async_computation.1 | async-start | bytes 2228224 | tf_op jit(solution)/shard_map/all_gather | solution.py:50
  9.4 140.1 %reduce-scatter.2.cloned.1.call-start = ((), (), s32[]{:S(2)}) async-start(), calls=%async_computation.2 | async-start | bytes 393216 | tf_op jit(solution)/shard_map/reduce_scatter | solution.py:57
  53.7 95.7 %copy-start.1 = (bf16[128,512]{1,0:T(8,128)(2,1)S(1)}, bf16[128,512]{1,0:T(8,128)(2,1)}, u32[]{:S(2)}) copy-start(bf16[128,512]{1,0:T(8,128)(2,1)} %param.11) | copy-start | bytes 393220
  53.8 95.7 %copy-start.2 = (bf16[512,512]{1,0:T(8,128)(2,1)S(1)}, bf16[512,512]{1,0:T(8,128)(2,1)}, u32[]{:S(2)}) copy-start(bf16[512,512]{1,0:T(8,128)(2,1)} %param.14) | copy-start | bytes 1572868
Sparse Core Ops, SparseCore 0:
  9.5 44.1 all-gather.1
  107.6 41.8 reduce-scatter.1
where the time goes:
time: 160 us; the launch traced here: 158 us
  waiting for transfers between devices  77.1 us (48%)
  local copies, waits for them, and re-layouts  26.9 us (17%)
  loops' own time  26.1 us (16%)
  between operations  14.1 us (9%)
  blocking collectives  7.09 us (4%)
  matrix products  6.07 us (4%)
    reduce_scatter x1, waiting for transfers between devices, on_device(): lax.psum_scatter(partial_value.astype(jnp.bfloat16), 'rep', scatter_dimen...  42 us
    all_gather x1, waiting for transfers between devices, on_device(): portion = lax.all_gather(key_rows, 'wide', axis=0, tiled=True)  35 us
    another operation x16, loops' own time, one_step(): lax.fori_loop(bounds[step_num], bounds[step_num + 1], lambda tile_num, ac...  25.1 us
    dynamic_slice x16, local copies, waits for them, and re-layouts, per_shard(): lax.dynamic_slice_in_dim(portion, index_in * tile_rows, tile_rows, 0)  14.6 us
    dynamic_slice x16, local copies, waits for them, and re-layouts, one_step(): bounds[step_num + 1]  10.5 us
    all_gather x1, blocking collectives, on_device(): receivers = lax.all_gather(query_rows, 'rep', axis=0, tiled=True)  7.09 us
  transfers between devices with their start and end apart: 2, of which 2 were waited for; matrix products, arithmetic and copies ran while one was open for 1% of the time, Pallas kernels for 0%

commit v1 on v0

v1 whole, which is shorter than its diff:
```python
import jax
import jax.numpy as jnp
from jax import lax
from jax.experimental import pallas as pl
from jax.experimental.pallas import tpu as pltpu
from jax.sharding import PartitionSpec as P

NT = (((1,), (1,)), ((), ()))


def xor_pairs(n, k):
    return [(i, i ^ k) for i in range(n)]


def gather_blocks(block, n_wide):
    def send(value, k):
        return lax.ppermute(value, "wide", xor_pairs(n_wide, k))

    held = {0: block}
    for k in range(4, n_wide, 4):
        held[k] = send(block, k)
    for k in list(held):
        held[k ^ 2] = send(held[k], 2)
    for k in list(held):
        held[k ^ 1] = send(held[k], 1)
    return held


def tiles_kernel(order, n_wide, n_rep, factor, slot_ref, count_ref, weight_ref, query_ref, *rest):
    blocks = rest[: len(order)]
    own_ref, others_ref, total, first, number = rest[len(order) :]
    wide_pos = lax.axis_index("wide")
    rep_pos = lax.axis_index("rep")
    for k in range(n_wide):
        number[k] = 0
        first[k] = 0

    def note(tile, carry):
        step = slot_ref[tile] // n_rep
        k = wide_pos ^ lax.rem(wide_pos - step + n_wide, n_wide)
        seen = number[k]
        first[k] = jnp.where(seen == 0, tile, first[k])
        number[k] = seen + 1
        return carry

    lax.fori_loop(0, count_ref[0], note, 0)
    total[...] = jnp.zeros_like(total)
    for k, block_ref in zip(order, blocks):

        def one_tile(tile, carry, block_ref=block_ref):
            part = lax.rem(lax.rem(slot_ref[tile], n_rep) - rep_pos + n_rep, n_rep)
            block = block_ref[...]
            scores = lax.dot_general(query_ref[part], block, NT, preferred_element_type=jnp.float32)
            weighted = jnp.tanh(scores * factor) * weight_ref[tile].astype(jnp.float32)
            total[part] += jnp.dot(
                weighted.astype(jnp.bfloat16), block, preferred_element_type=jnp.float32
            )
            return carry

        lax.fori_loop(first[k], first[k] + number[k], one_tile, 0)
    own_ref[...] = total[0]
    for part in range(1, n_rep):
        others_ref[part - 1] = total[part].astype(jnp.bfloat16)


def output_kernel(own_ref, w_key_ref, w_out_ref, features_ref, *rest):
    *received, out_ref = rest
    mixed = own_ref[...]
    for ref in received:
        mixed += ref[...].astype(jnp.float32)
    message = jnp.dot(
        mixed.astype(jnp.bfloat16), w_key_ref[...], preferred_element_type=jnp.float32
    ).astype(jnp.bfloat16)
    updated = features_ref[...].astype(jnp.float32) + jnp.dot(
        message, w_out_ref[...], preferred_element_type=jnp.float32
    )
    out_ref[...] = updated.astype(jnp.bfloat16)


def on_device(features, w_query, w_key, w_out, edge_weight, tile_slot, tile_count):
    rows, width = features.shape
    n_wide = lax.axis_size("wide")
    n_rep = lax.axis_size("rep")
    vmem = pl.BlockSpec(memory_space=pltpu.VMEM)
    smem = pl.BlockSpec(memory_space=pltpu.SMEM)

    held = gather_blocks(features, n_wide)
    queries = []
    for part in range(n_rep):
        block = features
        if part:
            block = lax.ppermute(
                features, "rep", [((i + part) % n_rep, i) for i in range(n_rep)]
            )
        query = jnp.dot(block, w_query, preferred_element_type=jnp.float32).astype(jnp.bfloat16)
        query = lax.dot_general(query, w_key, NT, preferred_element_type=jnp.float32)
        queries.append(query.astype(jnp.bfloat16))
    order = list(held)
    own, others = pl.pallas_call(
        lambda *refs: tiles_kernel(order, n_wide, n_rep, 1.0 / float(width) ** 0.5, *refs),
        out_shape=(
            jax.ShapeDtypeStruct((rows, width), jnp.float32),
            jax.ShapeDtypeStruct((n_rep - 1, rows, width), jnp.bfloat16),
        ),
        in_specs=[smem, smem] + [vmem] * (2 + len(order)),
        out_specs=(vmem, vmem),
        scratch_shapes=[
            pltpu.VMEM((n_rep, rows, width), jnp.float32),
            pltpu.SMEM((n_wide,), jnp.int32),
            pltpu.SMEM((n_wide,), jnp.int32),
        ],
        compiler_params=pltpu.CompilerParams(vmem_limit_bytes=48 << 20),
        name="tiles",
    )(
        tile_slot[0, 0],
        tile_count[0],
        edge_weight[0, 0],
        jnp.stack(queries),
        *[held[k] for k in order],
    )
    received = [
        lax.ppermute(others[part - 1], "rep", [(i, (i + part) % n_rep) for i in range(n_rep)])
        for part in range(1, n_rep)
    ]
    return pl.pallas_call(
        output_kernel,
        out_shape=jax.ShapeDtypeStruct((rows, width), jnp.bfloat16),
        in_specs=[vmem] * (4 + len(received)),
        out_specs=vmem,
        compiler_params=pltpu.CompilerParams(vmem_limit_bytes=32 << 20),
        name="output",
    )(own, w_key, w_out, features, *received)


def solution(mesh):
    in_specs = (
        P(("wide", "rep"), None),
        P(),
        P(),
        P(),
        P("wide", "rep", None, None, None),
        P("wide", "rep", None),
        P("wide", "rep"),
    )
    out_specs = P(("wide", "rep"), None)
    return jax.shard_map(
        on_device, mesh=mesh, in_specs=in_specs, out_specs=out_specs, check_vma=False
    )
```

time: 160 us -> 37.5 us (0.23)
  waiting for transfers between devices: 77.1 us -> 16.1 us
  local copies, waits for them, and re-layouts: 26.9 us -> 0.7 us
  loops' own time: 26.1 us -> 0 us
  between operations: 14.1 us -> 0.79 us
  starting transfers between devices: 0.04 us -> 13.2 us
  blocking collectives: 7.09 us -> 0 us
  Pallas kernels: 0 us -> 4.19 us
  matrix products: 6.07 us -> 1.99 us
    reduce_scatter x1 -> x0, waiting for transfers between devices: 42 us -> none  [on_device(): lax.psum_scatter(partial_value.astype(jnp.bfloat16), 'rep', scatter_dimen...]
    all_gather x1 -> x0, waiting for transfers between devices: 35 us -> none  [on_device(): portion = lax.all_gather(key_rows, 'wide', axis=0, tiled=True)]
    another operation x17 -> x0, loops' own time: 26.1 us -> none  [the longest x16 25.1 us: one_step(): lax.fori_loop(bounds[step_num], bounds[step_num + 1], lambda tile_num, ac...]
    dynamic_slice x33 -> x0, local copies, waits for them, and re-layouts: 25.8 us -> none  [the longest x16 14.6 us: per_shard(): lax.dynamic_slice_in_dim(portion, index_in * tile_rows, tile_rows, 0)]
    ppermute x0 -> x17, waiting for transfers between devices: none -> 16.1 us  [the longest x15 11.2 us: send(): return lax.ppermute(value, 'wide', xor_pairs(n_wide, k))]
    ppermute x0 -> x17, starting transfers between devices: none -> 13.2 us  [the longest x15 11.6 us: send(): return lax.ppermute(value, 'wide', xor_pairs(n_wide, k))]
    all_gather x1 -> x0, blocking collectives: 7.09 us -> none  [on_device(): receivers = lax.all_gather(query_rows, 'rep', axis=0, tiled=True)]
    pallas_call x0 -> x2, Pallas kernels: none -> 4.19 us  [the longest x1 3.11 us: on_device(): pl.pallas_call(lambda *refs: tiles_kernel(order, n_wide, n_rep, 1.0 / flo...]
  transfers between devices with their start and end apart: 2 -> 17, of which waited for: 2 -> 7; matrix products, arithmetic and copies ran while one was open for 1% -> 5% of each run, Pallas kernels for 0% -> 0%
where the time goes in v1:
time: 37.5 us; the launch traced here: 37 us
  waiting for transfers between devices  16.1 us (43%)
  starting transfers between devices  13.2 us (35%)
  Pallas kernels  4.19 us (11%)
  matrix products  1.99 us (5%)
  between operations  0.79 us (2%)
  local copies, waits for them, and re-layouts  0.7 us (2%)
    ppermute x15, starting transfers between devices, send(): return lax.ppermute(value, 'wide', xor_pairs(n_wide, k))  11.6 us
    ppermute x15, waiting for transfers between devices, send(): return lax.ppermute(value, 'wide', xor_pairs(n_wide, k))  11.2 us
    ppermute x1, waiting for transfers between devices, on_device(): lax.ppermute(others[part - 1], 'rep', [(i, (i + part) % n_rep) for i in r...  4.95 us
    pallas_call x1, Pallas kernels, on_device(): pl.pallas_call(lambda *refs: tiles_kernel(order, n_wide, n_rep, 1.0 / flo...  3.11 us
    dot_general x2, matrix products, on_device(): lax.dot_general(query, w_key, NT, preferred_element_type=jnp.float32)  1.99 us
    ppermute x1, starting transfers between devices, on_device(): lax.ppermute(features, 'rep', [((i + part) % n_rep, i) for i in range(n_r...  1.49 us
    pallas_call x1, Pallas kernels, on_device(): pl.pallas_call(output_kernel, out_shape=jax.ShapeDtypeStruct((rows, width...  1.08 us
  transfers between devices with their start and end apart: 17, of which 7 were waited for; matrix products, arithmetic and copies ran while one was open for 5% of the time, Pallas kernels for 0%

profile of v1, /device:TPU:0, one launch (start us, length us, event | category | flops | bytes accessed | tf_op | source)
XLA Modules:
  0.0 37.0 jit_solution(18047784388382701455)
XLA Ops:
  0.0 0.5 %collective-permute-start.8 = (bf16[128,512]{1,0:T(8,128)(2,1)}, bf16[128,512]{1,0:T(8,128)(2,1)S(1)}, u32[]{:S(2)}, u32[]{:S(2)}) collective-permute-start(bf16[128,512]{1,0:T(8,128)(2,1)} %features_ref.1), channel_id=1, source_target_pairs={{0,2},{2,0},{4,6},{6,4},{8,10},{10,8},{12,14},{14,12},{16,18},{18,... | collective-permute-start | bytes 393224 | tf_op jit(solution)/shard_map/ppermute | solution.py:17
  0.5 4.7 %collective-permute-start.3 = (bf16[128,512]{1,0:T(8,128)(2,1)}, bf16[128,512]{1,0:T(8,128)(2,1)S(1)}, u32[]{:S(2)}, u32[]{:S(2)}) collective-permute-start(bf16[128,512]{1,0:T(8,128)(2,1)} %features_ref.1), channel_id=1, source_target_pairs={{0,24},{2,26},{4,28},{6,30},{8,16},{10,18},{12,20},{14,22},{16,8},... | collective-permute-start | bytes 393224 | tf_op jit(solution)/shard_map/ppermute | solution.py:17
  5.1 1.5 %collective-permute-start.4 = (bf16[128,512]{1,0:T(8,128)(2,1)}, bf16[128,512]{1,0:T(8,128)(2,1)S(1)}, u32[]{:S(2)}, u32[]{:S(2)}) collective-permute-start(bf16[128,512]{1,0:T(8,128)(2,1)} %features_ref.1), channel_id=1, source_target_pairs={{0,4},{2,6},{4,0},{6,2},{8,12},{10,14},{12,8},{14,10},{16,20},{18,... | collective-permute-start | bytes 393224 | tf_op jit(solution)/shard_map/ppermute | solution.py:17
  6.6 0.8 %collective-permute-start.1 = (bf16[128,512]{1,0:T(8,128)(2,1)}, bf16[128,512]{1,0:T(8,128)(2,1)S(1)}, u32[]{:S(2)}, u32[]{:S(2)}) collective-permute-start(bf16[128,512]{1,0:T(8,128)(2,1)} %features_ref.1), channel_id=1, source_target_pairs={{0,8},{2,10},{4,12},{6,14},{8,0},{10,2},{12,4},{14,6},{16,24},{18,... | collective-permute-start | bytes 393224 | tf_op jit(solution)/shard_map/ppermute | solution.py:17
  7.4 1.5 %collective-permute-start = (bf16[128,512]{1,0:T(8,128)(2,1)}, bf16[128,512]{1,0:T(8,128)(2,1)S(1)}, u32[]{:S(2)}, u32[]{:S(2)}) collective-permute-start(bf16[128,512]{1,0:T(8,128)(2,1)} %features_ref.1), channel_id=1, source_target_pairs={{1,0},{0,1},{3,2},{2,3},{5,4},{4,5},{7,6},{6,7},{9,8},{8,9},{11,10... | collective-permute-start | bytes 393224 | tf_op jit(solution)/shard_map/ppermute | solution.py:92
  9.6 0.2 collective-permute-done.3.refs_7_
  9.8 1.1 %collective-permute-done.4.refs_8_ = bf16[128,512]{1,0:T(8,128)(2,1)S(1)} collective-permute-done((bf16[128,512]{1,0:T(8,128)(2,1)}, bf16[128,512]{1,0:T(8,128)(2,1)S(1)}, u32[]{:S(2)}, u32[]{:S(2)}) %collective-permute-start.4) | collective-permute-done | bytes 131104 | tf_op jit(solution)/shard_map/ppermute | solution.py:17
  10.9 1.5 %collective-permute-start.7 = (bf16[128,512]{1,0:T(8,128)(2,1)S(1)}, bf16[128,512]{1,0:T(8,128)(2,1)S(1)}, u32[]{:S(2)}, u32[]{:S(2)}) collective-permute-start(bf16[128,512]{1,0:T(8,128)(2,1)S(1)} %collective-permute-done.3.refs_7_), channel_id=1, source_target_pairs={{0,4},{2,6},{4,0},{6,2},{8,12},{10,14},{12,8},{14,10},{16,20},{18,... | collective-permute-start | bytes 393224 | tf_op jit(solution)/shard_map/ppermute | solution.py:17
  12.4 4.6 %collective-permute-done.2.refs_6_ = bf16[128,512]{1,0:T(8,128)(2,1)S(1)} collective-permute-done((bf16[128,512]{1,0:T(8,128)(2,1)}, bf16[128,512]{1,0:T(8,128)(2,1)S(1)}, u32[]{:S(2)}, u32[]{:S(2)}) %collective-permute-start.2) | collective-permute-done | bytes 131104 | tf_op jit(solution)/shard_map/ppermute | solution.py:17
  17.0 1.5 %collective-permute-start.6 = (bf16[128,512]{1,0:T(8,128)(2,1)S(1)}, bf16[128,512]{1,0:T(8,128)(2,1)S(1)}, u32[]{:S(2)}, u32[]{:S(2)}) collective-permute-start(bf16[128,512]{1,0:T(8,128)(2,1)S(1)} %collective-permute-done.2.refs_6_), channel_id=1, source_target_pairs={{0,4},{2,6},{4,0},{6,2},{8,12},{10,14},{12,8},{14,10},{16,20},{18,... | collective-permute-start | bytes 393224 | tf_op jit(solution)/shard_map/ppermute | solution.py:17
  18.5 0.5 %collective-permute-start.5 = (bf16[128,512]{1,0:T(8,128)(2,1)S(1)}, bf16[128,512]{1,0:T(8,128)(2,1)S(1)}, u32[]{:S(2)}, u32[]{:S(2)}) collective-permute-start(bf16[128,512]{1,0:T(8,128)(2,1)S(1)} %collective-permute-done.1.refs_5_), channel_id=1, source_target_pairs={{0,4},{2,6},{4,0},{6,2},{8,12},{10,14},{12,8},{14,10},{16,20},{18,... | collective-permute-start | bytes 393224 | tf_op jit(solution)/shard_map/ppermute | solution.py:17
  19.1 1.6 %fusion = bf16[1,128,512]{2,1,0:T(8,128)(2,1)S(1)} fusion(bf16[512,512]{1,0:T(8,128)(2,1)} %w_key_ref.1, bf16[128,512]{1,0:T(8,128)(2,1)} %features_ref.1, bf16[512,512]{1,0:T(8,128)(2,1)S(1)} %copy-done), kind=kOutput, calls=%fused_computation.4 | convolution fusion | flops 134348800 | bytes 1310720 | tf_op jit(solution)/shard_map/dot_general | solution.py:96
  20.6 0.1 collective-permute-start.10
  20.7 0.5 %collective-permute-start.9 = (bf16[128,512]{1,0:T(8,128)(2,1)S(1)}, bf16[128,512]{1,0:T(8,128)(2,1)S(1)}, u32[]{:S(2)}, u32[]{:S(2)}) collective-permute-start(bf16[128,512]{1,0:T(8,128)(2,1)S(1)} %collective-permute-done.1.refs_5_), channel_id=1, source_target_pairs={{0,2},{2,0},{4,6},{6,4},{8,10},{10,8},{12,14},{14,12},{16,18},{18,... | collective-permute-start | bytes 393224 | tf_op jit(solution)/shard_map/ppermute | solution.py:17
  21.2 0.1 collective-permute-start.15
  21.3 2.0 %collective-permute-done.6.refs_10_ = bf16[128,512]{1,0:T(8,128)(2,1)S(1)} collective-permute-done((bf16[128,512]{1,0:T(8,128)(2,1)S(1)}, bf16[128,512]{1,0:T(8,128)(2,1)S(1)}, u32[]{:S(2)}, u32[]{:S(2)}) %collective-permute-start.6) | collective-permute-done | bytes 131104 | tf_op jit(solution)/shard_map/ppermute | solution.py:17
  23.3 2.4 %collective-permute-done.5.refs_9_ = bf16[128,512]{1,0:T(8,128)(2,1)S(1)} collective-permute-done((bf16[128,512]{1,0:T(8,128)(2,1)S(1)}, bf16[128,512]{1,0:T(8,128)(2,1)S(1)}, u32[]{:S(2)}, u32[]{:S(2)}) %collective-permute-start.5) | collective-permute-done | bytes 131104 | tf_op jit(solution)/shard_map/ppermute | solution.py:17
  25.7 0.4 %fusion.1 = bf16[1,128,512]{2,1,0:T(8,128)(2,1)S(1)} fusion(bf16[512,512]{1,0:T(8,128)(2,1)S(1)} %copy-done.1, bf16[128,512]{1,0:T(8,128)(2,1)S(1)} %collective-permute-done, bf16[512,512]{1,0:T(8,128)(2,1)S(1)} %copy-done), kind=kOutput, calls=%fused_computation.5 | convolution fusion | flops 134348800 | bytes 1310720 | tf_op jit(solution)/shard_map/dot_general | solution.py:96
  26.3 0.8 %collective-permute-done.13.refs_17_ = bf16[128,512]{1,0:T(8,128)(2,1)S(1)} collective-permute-done((bf16[128,512]{1,0:T(8,128)(2,1)S(1)}, bf16[128,512]{1,0:T(8,128)(2,1)S(1)}, u32[]{:S(2)}, u32[]{:S(2)}) %collective-permute-start.13) | collective-permute-done | bytes 131104 | tf_op jit(solution)/shard_map/ppermute | solution.py:17
  27.1 0.1 copy-done.4
  27.2 0.6 %copy-done.5 = s32[1,1,6]{2,1,0:T(1,128)S(1)} copy-done((s32[1,1,6]{2,1,0:T(1,128)S(1)}, s32[1,1,6]{2,1,0:T(1,128)}, u32[]{:S(2)}) %copy-start.5) | copy-done | bytes 48
  27.8 3.1 %tiles.1 = (f32[128,512]{1,0:T(8,128)S(1)}, bf16[1,128,512]{2,1,0:T(8,128)(2,1)S(1)}) custom-call(s32[6]{0:T(128)S(1)} %bitcast.16, s32[1]{0:T(128)} %bitcast.14.refs_1_, bf16[6,128,128]{2,1,0:T(8,128)(2,1)S(1)} %bitcast.15, bf16[2,128,512]{2,1,0:T(8,128)(2,1)S(1)} %pad_maximum_fusion.refs_3_, bf16[128,512]{1,0:T(8,128)(2,1)S(1)} %copy-done.2, ...), custom_call_target="tpu_custom_call" | custom-call | tf_op jit(solution)/shard_map/tiles/pallas_call | solution.py:99
  31.0 5.0 %collective-permute-done.16.rest_0_ = bf16[128,512]{1,0:T(8,128)(2,1)S(1)} collective-permute-done((bf16[128,512]{1,0:T(8,128)(2,1)S(1)}, bf16[128,512]{1,0:T(8,128)(2,1)S(1)}, u32[]{:S(2)}, u32[]{:S(2)}) %collective-permute-start.16) | collective-permute-done | bytes 131104 | tf_op jit(solution)/shard_map/ppermute | solution.py:122
  35.9 1.1 %output.1 = bf16[128,512]{1,0:T(8,128)(2,1)} custom-call(f32[128,512]{1,0:T(8,128)S(1)} %get-tuple-element.7.own_ref, bf16[512,512]{1,0:T(8,128)(2,1)S(1)} %copy-done.1, bf16[512,512]{1,0:T(8,128)(2,1)S(1)} %copy-done.3, bf16[128,512]{1,0:T(8,128)(2,1)S(1)} %copy-done.2, bf16[128,512]{1,0:T(8,128)(2,1)S(1)} %collective-permute-done.16.rest_0_), custom_call_target="tpu_custom_call" | custom-call | tf_op jit(solution)/shard_map/output/pallas_call | solution.py:125
  (27 shorter events, 0.2 us)
Async XLA Ops:
  0.0 19.1 %copy-start = (bf16[512,512]{1,0:T(8,128)(2,1)S(1)}, bf16[512,512]{1,0:T(8,128)(2,1)}, u32[]{:S(2)}) copy-start(bf16[512,512]{1,0:T(8,128)(2,1)} %param.8) | copy-start | bytes 1572868
  0.0 7.4 %collective-permute-start.8 = (bf16[128,512]{1,0:T(8,128)(2,1)}, bf16[128,512]{1,0:T(8,128)(2,1)S(1)}, u32[]{:S(2)}, u32[]{:S(2)}) collective-permute-start(bf16[128,512]{1,0:T(8,128)(2,1)} %features_ref.1), channel_id=1, source_target_pairs={{0,2},{2,0},{4,6},{6,4},{8,10},{10,8},{12,14},{14,12},{16,18},{18,... | collective-permute-start | bytes 393224 | tf_op jit(solution)/shard_map/ppermute | solution.py:17
  0.5 9.3 %collective-permute-start.3 = (bf16[128,512]{1,0:T(8,128)(2,1)}, bf16[128,512]{1,0:T(8,128)(2,1)S(1)}, u32[]{:S(2)}, u32[]{:S(2)}) collective-permute-start(bf16[128,512]{1,0:T(8,128)(2,1)} %features_ref.1), channel_id=1, source_target_pairs={{0,24},{2,26},{4,28},{6,30},{8,16},{10,18},{12,20},{14,22},{16,8},... | collective-permute-start | bytes 393224 | tf_op jit(solution)/shard_map/ppermute | solution.py:17
  5.1 5.8 %collective-permute-start.4 = (bf16[128,512]{1,0:T(8,128)(2,1)}, bf16[128,512]{1,0:T(8,128)(2,1)S(1)}, u32[]{:S(2)}, u32[]{:S(2)}) collective-permute-start(bf16[128,512]{1,0:T(8,128)(2,1)} %features_ref.1), channel_id=1, source_target_pairs={{0,4},{2,6},{4,0},{6,2},{8,12},{10,14},{12,8},{14,10},{16,20},{18,... | collective-permute-start | bytes 393224 | tf_op jit(solution)/shard_map/ppermute | solution.py:17
  6.6 10.4 %collective-permute-start.2 = (bf16[128,512]{1,0:T(8,128)(2,1)}, bf16[128,512]{1,0:T(8,128)(2,1)S(1)}, u32[]{:S(2)}, u32[]{:S(2)}) collective-permute-start(bf16[128,512]{1,0:T(8,128)(2,1)} %features_ref.1), channel_id=1, source_target_pairs={{0,16},{2,18},{4,20},{6,22},{8,24},{10,26},{12,28},{14,30},{16,0},... | collective-permute-start | bytes 393224 | tf_op jit(solution)/shard_map/ppermute | solution.py:17
  6.6 10.4 %collective-permute-start.1 = (bf16[128,512]{1,0:T(8,128)(2,1)}, bf16[128,512]{1,0:T(8,128)(2,1)S(1)}, u32[]{:S(2)}, u32[]{:S(2)}) collective-permute-start(bf16[128,512]{1,0:T(8,128)(2,1)} %features_ref.1), channel_id=1, source_target_pairs={{0,8},{2,10},{4,12},{6,14},{8,0},{10,2},{12,4},{14,6},{16,24},{18,... | collective-permute-start | bytes 393224 | tf_op jit(solution)/shard_map/ppermute | solution.py:17
  7.4 11.1 %collective-permute-start = (bf16[128,512]{1,0:T(8,128)(2,1)}, bf16[128,512]{1,0:T(8,128)(2,1)S(1)}, u32[]{:S(2)}, u32[]{:S(2)}) collective-permute-start(bf16[128,512]{1,0:T(8,128)(2,1)} %features_ref.1), channel_id=1, source_target_pairs={{1,0},{0,1},{3,2},{2,3},{5,4},{4,5},{7,6},{6,7},{9,8},{8,9},{11,10... | collective-permute-start | bytes 393224 | tf_op jit(solution)/shard_map/ppermute | solution.py:92
  9.6 16.2 %copy-start.1 = (bf16[512,512]{1,0:T(8,128)(2,1)S(1)}, bf16[512,512]{1,0:T(8,128)(2,1)}, u32[]{:S(2)}) copy-start(bf16[512,512]{1,0:T(8,128)(2,1)} %w_key_ref.1) | copy-start | bytes 1572868
  9.8 10.9 %collective-permute-start.11 = (bf16[128,512]{1,0:T(8,128)(2,1)S(1)}, bf16[128,512]{1,0:T(8,128)(2,1)S(1)}, u32[]{:S(2)}, u32[]{:S(2)}) collective-permute-start(bf16[128,512]{1,0:T(8,128)(2,1)S(1)} %collective-permute-done.3.refs_7_), channel_id=1, source_target_pairs={{0,2},{2,0},{4,6},{6,4},{8,10},{10,8},{12,14},{14,12},{16,18},{18,... | collective-permute-start | bytes 393224 | tf_op jit(solution)/shard_map/ppermute | solution.py:17
  10.9 10.3 %collective-permute-start.7 = (bf16[128,512]{1,0:T(8,128)(2,1)S(1)}, bf16[128,512]{1,0:T(8,128)(2,1)S(1)}, u32[]{:S(2)}, u32[]{:S(2)}) collective-permute-start(bf16[128,512]{1,0:T(8,128)(2,1)S(1)} %collective-permute-done.3.refs_7_), channel_id=1, source_target_pairs={{0,4},{2,6},{4,0},{6,2},{8,12},{10,14},{12,8},{14,10},{16,20},{18,... | collective-permute-start | bytes 393224 | tf_op jit(solution)/shard_map/ppermute | solution.py:17
  17.0 3.6 %collective-permute-start.12 = (bf16[128,512]{1,0:T(8,128)(2,1)S(1)}, bf16[128,512]{1,0:T(8,128)(2,1)S(1)}, u32[]{:S(2)}, u32[]{:S(2)}) collective-permute-start(bf16[128,512]{1,0:T(8,128)(2,1)S(1)} %collective-permute-done.4.refs_8_), channel_id=1, source_target_pairs={{0,2},{2,0},{4,6},{6,4},{8,10},{10,8},{12,14},{14,12},{16,18},{18,... | collective-permute-start | bytes 393224 | tf_op jit(solution)/shard_map/ppermute | solution.py:17
  17.0 6.3 %collective-permute-start.6 = (bf16[128,512]{1,0:T(8,128)(2,1)S(1)}, bf16[128,512]{1,0:T(8,128)(2,1)S(1)}, u32[]{:S(2)}, u32[]{:S(2)}) collective-permute-start(bf16[128,512]{1,0:T(8,128)(2,1)S(1)} %collective-permute-done.2.refs_6_), channel_id=1, source_target_pairs={{0,4},{2,6},{4,0},{6,2},{8,12},{10,14},{12,8},{14,10},{16,20},{18,... | collective-permute-start | bytes 393224 | tf_op jit(solution)/shard_map/ppermute | solution.py:17
  18.5 7.2 %collective-permute-start.5 = (bf16[128,512]{1,0:T(8,128)(2,1)S(1)}, bf16[128,512]{1,0:T(8,128)(2,1)S(1)}, u32[]{:S(2)}, u32[]{:S(2)}) collective-permute-start(bf16[128,512]{1,0:T(8,128)(2,1)S(1)} %collective-permute-done.1.refs_5_), channel_id=1, source_target_pairs={{0,4},{2,6},{4,0},{6,2},{8,12},{10,14},{12,8},{14,10},{16,20},{18,... | collective-permute-start | bytes 393224 | tf_op jit(solution)/shard_map/ppermute | solution.py:17
  20.6 5.6 %collective-permute-start.10 = (bf16[128,512]{1,0:T(8,128)(2,1)S(1)}, bf16[128,512]{1,0:T(8,128)(2,1)S(1)}, u32[]{:S(2)}, u32[]{:S(2)}) collective-permute-start(bf16[128,512]{1,0:T(8,128)(2,1)S(1)} %collective-permute-done.2.refs_6_), channel_id=1, source_target_pairs={{0,2},{2,0},{4,6},{6,4},{8,10},{10,8},{12,14},{14,12},{16,18},{18,... | collective-permute-start | bytes 393224 | tf_op jit(solution)/shard_map/ppermute | solution.py:17
  20.7 5.6 %collective-permute-start.9 = (bf16[128,512]{1,0:T(8,128)(2,1)S(1)}, bf16[128,512]{1,0:T(8,128)(2,1)S(1)}, u32[]{:S(2)}, u32[]{:S(2)}) collective-permute-start(bf16[128,512]{1,0:T(8,128)(2,1)S(1)} %collective-permute-done.1.refs_5_), channel_id=1, source_target_pairs={{0,2},{2,0},{4,6},{6,4},{8,10},{10,8},{12,14},{14,12},{16,18},{18,... | collective-permute-start | bytes 393224 | tf_op jit(solution)/shard_map/ppermute | solution.py:17
  21.2 5.1 %collective-permute-start.15 = (bf16[128,512]{1,0:T(8,128)(2,1)S(1)}, bf16[128,512]{1,0:T(8,128)(2,1)S(1)}, u32[]{:S(2)}, u32[]{:S(2)}) collective-permute-start(bf16[128,512]{1,0:T(8,128)(2,1)S(1)} %collective-permute-done.7.refs_11_), channel_id=1, source_target_pairs={{0,2},{2,0},{4,6},{6,4},{8,10},{10,8},{12,14},{14,12},{16,18},{18,... | collective-permute-start | bytes 393224 | tf_op jit(solution)/shard_map/ppermute | solution.py:17
  23.3 3.0 %collective-permute-start.14 = (bf16[128,512]{1,0:T(8,128)(2,1)S(1)}, bf16[128,512]{1,0:T(8,128)(2,1)S(1)}, u32[]{:S(2)}, u32[]{:S(2)}) collective-permute-start(bf16[128,512]{1,0:T(8,128)(2,1)S(1)} %collective-permute-done.6.refs_10_), channel_id=1, source_target_pairs={{0,2},{2,0},{4,6},{6,4},{8,10},{10,8},{12,14},{14,12},{16,18},{18,... | collective-permute-start | bytes 393224 | tf_op jit(solution)/shard_map/ppermute | solution.py:17
  25.7 1.3 %collective-permute-start.13 = (bf16[128,512]{1,0:T(8,128)(2,1)S(1)}, bf16[128,512]{1,0:T(8,128)(2,1)S(1)}, u32[]{:S(2)}, u32[]{:S(2)}) collective-permute-start(bf16[128,512]{1,0:T(8,128)(2,1)S(1)} %collective-permute-done.5.refs_9_), channel_id=1, source_target_pairs={{0,2},{2,0},{4,6},{6,4},{8,10},{10,8},{12,14},{14,12},{16,18},{18,... | collective-permute-start | bytes 393224 | tf_op jit(solution)/shard_map/ppermute | solution.py:17
  26.2 0.9 %copy-start.2 = (bf16[128,512]{1,0:T(8,128)(2,1)S(1)}, bf16[128,512]{1,0:T(8,128)(2,1)}, u32[]{:S(2)}) copy-start(bf16[128,512]{1,0:T(8,128)(2,1)} %features_ref.1) | copy-start | bytes 393220
  26.2 1.0 %copy-start.4 = (bf16[1,1,6,128,128]{4,3,2,1,0:T(8,128)(2,1)S(1)}, bf16[1,1,6,128,128]{4,3,2,1,0:T(8,128)(2,1)}, u32[]{:S(2)}) copy-start(bf16[1,1,6,128,128]{4,3,2,1,0:T(8,128)(2,1)} %param.11) | copy-start | bytes 589828
  27.1 0.7 %copy-start.5 = (s32[1,1,6]{2,1,0:T(1,128)S(1)}, s32[1,1,6]{2,1,0:T(1,128)}, u32[]{:S(2)}) copy-start(s32[1,1,6]{2,1,0:T(1,128)} %param.12) | copy-start | bytes 76
  27.8 8.2 %copy-start.3 = (bf16[512,512]{1,0:T(8,128)(2,1)S(1)}, bf16[512,512]{1,0:T(8,128)(2,1)}, u32[]{:S(2)}) copy-start(bf16[512,512]{1,0:T(8,128)(2,1)} %w_out_ref.1) | copy-start | bytes 1572868
  30.9 5.0 %collective-permute-start.16 = (bf16[128,512]{1,0:T(8,128)(2,1)S(1)}, bf16[128,512]{1,0:T(8,128)(2,1)S(1)}, u32[]{:S(2)}, u32[]{:S(2)}) collective-permute-start(bf16[128,512]{1,0:T(8,128)(2,1)S(1)} %bitcast.17), channel_id=1, source_target_pairs={{0,1},{1,0},{2,3},{3,2},{4,5},{5,4},{6,7},{7,6},{8,9},{9,8},{10,11... | collective-permute-start | bytes 393224 | tf_op jit(solution)/shard_map/ppermute | solution.py:122
